TPU v7x, 32 devices: a whole 2x2x4 slice. The times are simulated.
32 devices in a mesh: pair: 2 (over core), virt: 4 (over y, x), integ: 4 (over z).
Axes of the slice: x: 2, y: 2, z: 4, core: 2. Of those that a mesh axis runs over, the one named last changes fastest.
Arguments:
- amplitudes: bfloat16 [2, 4, 256, 256], P('pair', 'integ', 'virt'), may hold values from -4 to 4
- vv_factors: bfloat16 [64, 256, 256], P('integ'), may hold values from -0.25 to 0.25
- ov_factors: bfloat16 [64, 4, 256], P(None, 'integ'), may hold values from -0.75 to 0.75
- occ_energy_i: float32 [2], P('pair'), may hold values from -2 to -0.5
- occ_energy_j: float32 [4], P('integ'), may hold values from -2 to -0.5
- virt_energy: float32 [256], replicated, may hold values from 0.2 to 3
- vv_mask: int32 [2, 2], replicated, may hold values 0 or 1
- pair_domain: int32 [2, 4, 2], P('pair', 'integ'), may hold values 0 or 1
Outputs:
- update: bfloat16 [2, 4, 256, 256], P('pair', 'integ', 'virt')
All inputs are finite; a program needn't handle non-finite values. No bound on the sum of `pair_domain` on one device may be relied on, other than what follows from the above.
Results may differ from a plain program's by a relative error of at most 0.014.
Values may be sent and summed in bfloat16 or wider, within the bound.
A program may use at most 64 MiB of HBM per device.

v0:
```python
import jax
import jax.numpy as jnp
from jax import lax
from jax.sharding import PartitionSpec as P

TILE_SIZE = 128


def split_halves(values):
    upper = values.astype(jnp.bfloat16)
    lower = (values - upper.astype(jnp.float32)).astype(jnp.bfloat16)
    return (upper, lower)


def body(
    amplitudes,
    vv_factors,
    ov_factors,
    occ_energy_i,
    occ_energy_j,
    virt_energy,
    vv_mask,
    pair_domain,
):
    share = amplitudes.shape[2]
    virt_index = lax.axis_index("virt")
    row_start = virt_index * share
    domain = jnp.repeat(pair_domain[0, 0], TILE_SIZE).astype(jnp.float32)
    domain_rows = lax.dynamic_slice_in_dim(domain, row_start, share, 0)
    masked = (amplitudes[0, 0].astype(jnp.float32) * domain_rows[:, None] * domain[None, :]).astype(
        jnp.bfloat16
    )
    grid = jnp.repeat(jnp.repeat(vv_mask, TILE_SIZE, axis=0), TILE_SIZE, axis=1).astype(
        jnp.bfloat16
    )
    factors = vv_factors * grid[None]
    factor_rows = lax.dynamic_slice_in_dim(factors, row_start, share, 1)
    masked_block = masked[None, None]
    full_rows = lax.all_gather(masked_block, "virt", axis=2, tiled=True)
    own_pair = full_rows[0, 0]
    all_pairs = lax.all_gather(full_rows, "integ", axis=1, tiled=True)[0]
    columns = lax.dynamic_slice_in_dim(own_pair, row_start, share, 1)
    mixed = (2.0 * masked.astype(jnp.float32) - columns.T.astype(jnp.float32)).astype(jnp.bfloat16)
    own_ov = ov_factors[:, 0, :]
    partial_zeta = jnp.einsum("ac,qc->aq", mixed, own_ov, preferred_element_type=jnp.float32)
    pieces = []
    for first in range(0, lax.axis_size("integ") * 1, 8):
        width = min(8, lax.axis_size("integ") * 1 - first)
        block = lax.dynamic_slice_in_dim(all_pairs, first, width, 0)
        weighted = jnp.einsum(
            "qac,jcd->jqad", factor_rows, block, preferred_element_type=jnp.float32
        ).astype(jnp.bfloat16)
        pieces.append(
            jnp.einsum("jqad,qbd->jab", weighted, factors, preferred_element_type=jnp.float32)
        )
    term = jnp.concatenate(pieces, axis=0)
    ladder = lax.psum_scatter(
        term.astype(jnp.bfloat16), "integ", scatter_dimension=0, tiled=True
    ).astype(jnp.float32)[0]
    zeta = lax.psum(partial_zeta, "integ")
    upper, lower = split_halves(zeta)
    cycle = jnp.dot(upper, own_ov, preferred_element_type=jnp.float32)
    cycle = cycle + jnp.dot(lower, own_ov, preferred_element_type=jnp.float32)
    total = ladder + cycle
    energy_rows = lax.dynamic_slice_in_dim(virt_energy, row_start, share, 0)
    denom = energy_rows[:, None] + virt_energy[None, :] - occ_energy_i[0] - occ_energy_j[0]
    update = (total * domain_rows[:, None] * domain[None, :] / denom).astype(jnp.bfloat16)
    return update[None, None]


def solution(mesh):
    placed = (
        P("pair", "integ", "virt", None),
        P("integ", None, None),
        P(None, "integ", None),
        P("pair"),
        P("integ"),
        P(),
        P(),
        P("pair", "integ", None),
    )
    return jax.shard_map(
        body,
        mesh=mesh,
        in_specs=placed,
        out_specs=P("pair", "integ", "virt", None),
        check_vma=False,
    )
```

profile of v0, /device:TPU:0, one launch (start us, length us, event | category | flops | bytes accessed | tf_op | source)
XLA Modules:
  0.0 68.3 jit_solution(1602986020244581460)
XLA Ops:
  6.5 0.0 copy-start
  6.5 0.0 reduce-scatter.2.cloned.1.call-start
  6.5 0.7 convert_bitcast_fusion.2
  7.2 0.1 broadcast_bitcast_fusion
  7.3 0.1 dynamic_slice.12
  7.4 0.8 %fusion.29 = bf16[1,1,64,256]{3,2,1,0:T(8,128)(2,1)S(1)} fusion(bf16[1,1,64,256]{3,2,1,0:T(8,128)(2,1)} %param.8, f32[256]{0:T(256)S(1)} %broadcast_bitcast_fusion, f32[64]{0:T(128)S(1)} %dynamic_slice.12), kind=kLoop, calls=%fused_computation.22 | loop fusion | flops 65536 | bytes 66816 | tf_op jit(solution)/shard_map/convert_element_type | solution.py:30
  8.2 9.9 %all_gather.6 = bf16[1,1,256,256]{3,2,1,0:T(8,128)(2,1)S(1)} all-gather(bf16[1,1,64,256]{3,2,1,0:T(8,128)(2,1)S(1)} %fusion.29), channel_id=1, replica_groups=mesh['pair'=2,'virt'=4,'integ'=4] {'virt'}, dimensions={2}, use_global_device_ids=true | all-gather | bytes 163840 | tf_op jit(solution)/shard_map/all_gather | solution.py:39
  18.1 16.1 %all_gather.7 = bf16[1,4,256,256]{3,2,0,1:T(8,128)(2,1)S(1)} all-gather(bf16[1,1,256,256]{3,2,0,1:T(8,128)(2,1)S(1)} %bitcast.80), channel_id=1, replica_groups=mesh['pair'=2,'virt'=4,'integ'=4] {'integ'}, dimensions={1}, use_global_device_ids=true | all-gather | bytes 655360 | tf_op jit(solution)/shard_map/all_gather | solution.py:41
  34.2 0.7 convert_element_type.86
  34.9 0.3 broadcast_in_dim.10
  35.2 1.8 %broadcast_multiply_fusion = bf16[16,256,256]{2,1,0:T(8,128)(2,1)S(1)} fusion(bf16[16,256,256]{2,1,0:T(8,128)(2,1)} %param.9, bf16[256,256]{1,0:T(8,128)(2,1)S(1)} %bitcast.81), kind=kLoop, calls=%fused_computation.14 | loop fusion | flops 1048576 | bytes 4325376 | tf_op jit(solution)/shard_map/mul | solution.py:36
  37.0 0.0 copy-start.1
  37.0 0.0 copy-start.2
  37.0 2.8 %fusion.11 = bf16[4,64,256]{2,1,0:T(8,128)(2,1)} fusion(bf16[16,256,256]{2,1,0:T(8,128)(2,1)S(1)} %broadcast_multiply_fusion, bf16[1,4,256,256]{3,2,0,1:T(8,128)(2,1)S(1)} %all_gather.7, s32[]{:T(128)S(6)} %select_n.2), kind=kOutput, calls=%fused_computation.6 | convolution fusion | flops 1074855936 | bytes 3276804 | tf_op jit(solution)/shard_map/jqad,qbd->jab/dot_general | solution.py:54
  39.8 0.0 reduce-scatter.2.cloned.1.call-update
  39.8 0.1 constant_dynamic-slice_fusion
  39.9 0.1 copy.16
  40.0 0.0 copy-done
  40.0 0.0 copy-done.1
  40.0 0.2 fusion.35
  40.2 0.0 copy-done.2
  40.2 0.1 dynamic_slice.15
  41.6 18.2 %psum.7 = f32[64,64]{1,0:T(8,128)S(1)} all-reduce(f32[64,64]{1,0:T(8,128)S(1)} %fusion.35), channel_id=1, replica_groups=mesh['pair'=2,'virt'=4,'integ'=4] {'integ'}, use_global_device_ids=true, to_apply=%region_1.0 | all-reduce | flops 4096 | bytes 32768 | tf_op jit(solution)/shard_map/psum | solution.py:60
  59.9 0.1 fusion.40
  60.0 0.0 reduce-scatter.2.cloned.1.call-done
  60.0 1.5 %fusion.21 = bf16[1,1,64,256]{3,2,1,0:T(8,128)(2,1)} fusion(f32[64,256]{1,0:T(8,128)S(1)} %fusion.40, bf16[1,64,256]{2,1,0:T(8,128)(2,1)} %reduce-scatter.2.cloned.1.call-done, bf16[64,1,256]{2,0,1:T(8,128)(2,1)S(1)} %copy-done, f32[]{:T(128)} %bitcast.79, f32[]{:T(128)} %bitcast.78, f32[256]{0:T(256)S(1)} %copy-done.2, f32[64]{0:T(128)S(1)} %dynamic_slice.15, ...), kind=kOutput, calls=%fused_computation.13 | convolution fusion | flops 2277376 | bytes 182792 | tf_op jit(solution)/shard_map/dot_general | solution.py:63
  (2 shorter events, 0.0 us)
Async XLA Ops:
  6.5 33.5 %copy-start = (bf16[64,1,256]{2,0,1:T(8,128)(2,1)S(1)}, bf16[64,1,256]{2,0,1:T(8,128)(2,1)}, u32[]{:S(2)}) copy-start(bf16[64,1,256]{2,0,1:T(8,128)(2,1)} %param.10) | copy-start | bytes 98308
  6.5 53.4 %reduce-scatter.2.cloned.1.call-start = ((), (), s32[]{:S(2)}) async-start(), calls=%async_computation.1 | async-start | bytes 163840 | tf_op jit(solution)/shard_map/reduce_scatter | solution.py:57
  37.0 3.0 %copy-start.1 = (bf16[1,1,64,256]{3,2,1,0:T(8,128)(2,1)S(1)}, bf16[1,1,64,256]{3,2,1,0:T(8,128)(2,1)}, u32[]{:S(2)}) copy-start(bf16[1,1,64,256]{3,2,1,0:T(8,128)(2,1)} %param.8) | copy-start | bytes 98308
  37.0 3.2 %copy-start.2 = (f32[256]{0:T(256)S(1)}, f32[256]{0:T(256)}, u32[]{:S(2)}) copy-start(f32[256]{0:T(256)} %param.13) | copy-start | bytes 3076
Sparse Core Ops, SparseCore 0:
  40.0 18.4 reduce-scatter.1
where the time goes:
time: 68.8 us; the launch traced here: 68.3 us
  blocking collectives  44.2 us (64%)
  between operations  14.8 us (22%)
  matrix products  4.6 us (7%)
  other arithmetic  3.96 us (6%)
  local copies, waits for them, and re-layouts  0.8 us (1%)
    psum x1, blocking collectives, body(): zeta = lax.psum(partial_zeta, 'integ')  18.2 us
    all_gather x1, blocking collectives, body(): all_pairs = lax.all_gather(full_rows, 'integ', axis=1, tiled=True)[0]  16.1 us
    all_gather x1, blocking collectives, body(): full_rows = lax.all_gather(masked_block, 'virt', axis=2, tiled=True)  9.92 us
    dot_general x1, matrix products, body(): jnp.einsum('jqad,qbd->jab', weighted, factors, preferred_element_type=jnp...  2.77 us
    mul x1, other arithmetic, body(): factors = vv_factors * grid[None]  1.78 us
    dot_general x1, matrix products, body(): cycle = cycle + jnp.dot(lower, own_ov, preferred_element_type=jnp.float32)  1.52 us
  transfers between devices with their start and end apart: 1, of which 0 were waited for; matrix products, arithmetic and copies ran while one was open for 1% of the time, Pallas kernels for 0%

commit v1 on v0

v1 whole, which is shorter than its diff:
```python
import functools

import jax
import jax.numpy as jnp
from jax import lax
from jax.experimental import pallas as pl
from jax.experimental.pallas import tpu as pltpu
from jax.sharding import PartitionSpec as P

TILE_SIZE = 128
GROUP = 4
MESH = pl.DeviceIdType.MESH
F32 = jnp.float32
BF16 = jnp.bfloat16


def dot_nn(left, right):
    return lax.dot_general(left, right, (((1,), (0,)), ((), ())), preferred_element_type=F32)


def dot_nt(left, right):
    return lax.dot_general(left, right, (((1,), (1,)), ((), ())), preferred_element_type=F32)


def over_tiles(index, values):
    picked = jnp.zeros(index.shape, F32)
    for tile, value in enumerate(values):
        picked = jnp.where(index // TILE_SIZE == tile, value, picked)
    return picked


def kernel(
    columns,
    planes,
    amp_ref,
    ov_ref,
    occ_i_ref,
    occ_j_ref,
    energy_ref,
    vv_mask_ref,
    domain_ref,
    vv_ref,
    out_ref,
    factors,
    lines,
    pairs,
    ov_mine,
    zetas,
    terms,
    parts,
    load_sem,
    line_send,
    line_recv,
    pair_send,
    pair_recv,
    ov_send,
    ov_recv,
    zeta_send,
    zeta_recv,
    part_send,
    part_recv,
):
    pair = lax.axis_index("pair")
    virt = lax.axis_index("virt")
    integ = lax.axis_index("integ")
    share, wide = amp_ref.shape[2], amp_ref.shape[3]
    aux = vv_ref.shape[0]
    tiles = wide // TILE_SIZE
    held = planes // columns
    home = integ // held
    slot = integ % held

    def remote(src, dst, send_sem, recv_sem, to_virt, to_integ):
        return pltpu.make_async_remote_copy(
            src_ref=src,
            dst_ref=dst,
            send_sem=send_sem,
            recv_sem=recv_sem,
            device_id=(pair, to_virt, to_integ),
            device_id_type=MESH,
        )

    def rows(which):
        return pl.ds(pl.multiple_of(which * share, share), share)

    load = pltpu.make_async_copy(vv_ref, factors, load_sem)
    load.start()

    barrier = pltpu.get_barrier_semaphore()

    def greet(to_virt, to_integ):
        pl.semaphore_signal(
            barrier, inc=1, device_id=(pair, to_virt, to_integ), device_id_type=MESH
        )

    for step in range(1, planes):
        greet(virt, lax.rem(integ + step, planes))
    for step in range(1, columns):
        greet(lax.rem(virt + step, columns), integ)

    @pl.when(home != virt)
    def _():
        for step in range(1, planes):
            greet(home, lax.rem(integ + step, planes))

    domain = [domain_ref[0, 0, tile].astype(F32) for tile in range(tiles)]
    row_index = virt * share + lax.broadcasted_iota(jnp.int32, (share, wide), 0)
    col_index = lax.broadcasted_iota(jnp.int32, (share, wide), 1)
    pair_mask = over_tiles(row_index, domain) * over_tiles(col_index, domain)
    lines[integ] = (amp_ref[0, 0].astype(F32) * pair_mask).astype(BF16)

    own_home = jnp.where(home == virt, 1, 0)
    pl.semaphore_wait(barrier, planes - 1 + (columns - 1) * (held + 1 - own_home))

    def line_copy(step):
        return remote(
            lines.at[integ],
            lines.at[integ],
            line_send.at[step],
            line_recv.at[integ],
            virt,
            lax.rem(integ + step, planes),
        )

    def ov_copy(step):
        to_integ = lax.rem(integ + step, planes)
        return remote(
            ov_ref.at[pl.ds(pl.multiple_of(to_integ * aux, aux), aux)],
            ov_mine.at[slot],
            ov_send.at[step],
            ov_recv.at[slot],
            virt,
            to_integ,
        )

    def pair_copy(which):
        return remote(
            lines.at[which],
            pairs.at[which % held, rows(virt)],
            pair_send.at[which],
            pair_recv.at[(which % held) * columns + virt],
            which // held,
            integ,
        )

    def forward(which):
        @pl.when(which // held != virt)
        def _():
            pair_copy(which).start()

        @pl.when(which // held == virt)
        def _():
            pairs[which % held, rows(virt)] = lines[which]

    for step in range(1, planes):
        line_copy(step).start()
    forward(integ)

    @pl.when(home == virt)
    def _():
        for step in range(1, planes):
            ov_copy(step).start()
        ov_mine[slot] = ov_ref[pl.ds(pl.multiple_of(integ * aux, aux), aux)]

    row_in = lax.broadcasted_iota(jnp.int32, (wide, wide), 0) // TILE_SIZE
    col_in = lax.broadcasted_iota(jnp.int32, (wide, wide), 1) // TILE_SIZE
    grid = jnp.zeros((wide, wide), F32)
    for first in range(tiles):
        for second in range(tiles):
            here = jnp.logical_and(row_in == first, col_in == second)
            grid = jnp.where(here, vv_mask_ref[first, second].astype(F32), grid)
    grid = grid.astype(BF16)
    energy = jnp.broadcast_to(energy_ref[...], (share, wide))
    energy_rows = jnp.sum(jnp.where(col_index == row_index, energy, 0.0), axis=1, keepdims=True)
    denom = energy_rows + energy - occ_i_ref[0] - occ_j_ref[0]
    scale = pair_mask / denom
    load.wait()

    @pl.loop(0, aux)
    def _(q):
        factors[q] = factors[q] * grid

    for step in range(1, planes):
        which = lax.rem(integ + step, planes)
        line_copy_in = remote(
            lines.at[which], lines.at[which], line_send.at[step], line_recv.at[which], virt, which
        )
        line_copy_in.wait_recv()
        forward(which)

    for first in range(held):
        @pl.when(jnp.logical_or(home != virt, slot != first))
        def _(first=first):
            ov_in = remote(
                ov_mine.at[first], ov_mine.at[first], ov_send.at[0], ov_recv.at[first], virt, integ
            )
            ov_in.wait_recv()

        for step in range(1, columns):
            source = lax.rem(virt + step, columns)
            landed = pairs.at[first, rows(source)]
            remote(
                landed,
                landed,
                pair_send.at[0],
                pair_recv.at[first * columns + source],
                source,
                integ,
            ).wait_recv()

    zeta_part = jnp.zeros((aux, wide), F32)
    for first in range(held):
        amps = pairs[first]
        zeta_part += 2.0 * dot_nt(ov_mine[first], amps) - dot_nn(ov_mine[first], amps)
    zetas[virt] = zeta_part

    def zeta_copy(step):
        return remote(
            zetas.at[virt],
            zetas.at[virt],
            zeta_send.at[step],
            zeta_recv.at[virt],
            lax.rem(virt + step, columns),
            integ,
        )

    for step in range(1, columns):
        zeta_copy(step).start()

    def ladder(first):
        amps = pairs[first]

        def add(group, total):
            block = factors[pl.ds(group * GROUP, GROUP)]
            weighted = dot_nn(block.reshape(GROUP * wide, wide), amps).astype(BF16)
            for q in range(GROUP):
                total = total + dot_nt(weighted[q * wide:(q + 1) * wide], block[q])
            return total

        return lax.fori_loop(0, aux // GROUP, add, jnp.zeros((wide, wide), F32))

    def cycle(first, upper, lower):
        return dot_nn(upper, ov_mine[first]) + dot_nn(lower, ov_mine[first])

    def zeta_halves():
        for step in range(1, columns):
            source = lax.rem(virt + step, columns)
            landed = zetas.at[source]
            remote(
                landed, landed, zeta_send.at[0], zeta_recv.at[source], source, integ
            ).wait_recv()
        zeta = zetas[0]
        for column in range(1, columns):
            zeta = zeta + zetas[column]
        zeta = zeta.T
        upper = zeta.astype(BF16)
        return upper, (zeta - upper.astype(F32)).astype(BF16)

    def part_copy(first, row):
        return remote(
            terms.at[first, pl.ds(row * share, share)],
            parts.at[integ],
            part_send.at[first * columns + row],
            part_recv.at[integ],
            row,
            virt * held + first,
        )

    def hand_over(first):
        for row in range(columns):
            mine = jnp.logical_and(virt == row, virt * held + first == integ)

            @pl.when(jnp.logical_not(mine))
            def _(row=row):
                part_copy(first, row).start()

            @pl.when(mine)
            def _(row=row):
                parts[integ] = terms[first, pl.ds(row * share, share)]

    if held == 1:
        total = ladder(0)
        upper, lower = zeta_halves()
        terms[0] = (total + cycle(0, upper, lower)).astype(BF16)
        hand_over(0)
    else:
        upper, lower = zeta_halves()

        @pl.loop(0, held)
        def _(first):
            terms[first] = (ladder(first) + cycle(first, upper, lower)).astype(BF16)
            hand_over(first)

    for source in range(planes):
        @pl.when(jnp.logical_or(home != virt, integ != source))
        def _(source=source):
            remote(
                parts.at[source],
                parts.at[source],
                part_send.at[0],
                part_recv.at[source],
                home,
                integ,
            ).wait_recv()

    total = parts[0].astype(F32)
    for source in range(1, planes):
        total = total + parts[source].astype(F32)
    out_ref[0, 0] = (total * scale).astype(BF16)

    for step in range(1, planes):
        line_copy(step).wait_send()
    for step in range(1, columns):
        zeta_copy(step).wait_send()
    for which in range(planes):
        @pl.when(which // held != virt)
        def _(which=which):
            pair_copy(which).wait_send()

    @pl.when(home == virt)
    def _():
        for step in range(1, planes):
            ov_copy(step).wait_send()

    for first in range(held):
        for row in range(columns):
            mine = jnp.logical_and(virt == row, virt * held + first == integ)

            @pl.when(jnp.logical_not(mine))
            def _(first=first, row=row):
                part_copy(first, row).wait_send()


def body(
    columns,
    planes,
    amplitudes,
    vv_factors,
    ov_factors,
    occ_energy_i,
    occ_energy_j,
    virt_energy,
    vv_mask,
    pair_domain,
):
    share, wide = amplitudes.shape[2:]
    aux = vv_factors.shape[0]
    held = planes // columns
    vmem = pl.BlockSpec(memory_space=pltpu.VMEM)
    smem = pl.BlockSpec(memory_space=pltpu.SMEM)
    dma = pltpu.SemaphoreType.DMA
    return pl.pallas_call(
        functools.partial(kernel, columns, planes),
        out_shape=jax.ShapeDtypeStruct(amplitudes.shape, BF16),
        in_specs=[vmem, vmem, smem, smem, vmem, smem, smem, pl.BlockSpec(memory_space=pl.ANY)],
        out_specs=vmem,
        scratch_shapes=[
            pltpu.VMEM((aux, wide, wide), BF16),
            pltpu.VMEM((planes, share, wide), BF16),
            pltpu.VMEM((held, wide, wide), BF16),
            pltpu.VMEM((held, aux, wide), BF16),
            pltpu.VMEM((columns, aux, wide), F32),
            pltpu.VMEM((held, wide, wide), BF16),
            pltpu.VMEM((planes, share, wide), BF16),
            dma,
            dma((planes,)),
            dma((planes,)),
            dma((planes,)),
            dma((planes,)),
            dma((planes,)),
            dma((held,)),
            dma((columns,)),
            dma((columns,)),
            dma((planes,)),
            dma((planes,)),
        ],
        compiler_params=pltpu.CompilerParams(
            collective_id=0, has_side_effects=True, vmem_limit_bytes=40 * 1024 * 1024
        ),
        cost_estimate=pl.CostEstimate(
            flops=4 * held * aux * wide**3, bytes_accessed=2 * aux * wide * wide, transcendentals=0
        ),
    )(
        amplitudes,
        ov_factors.reshape(ov_factors.shape[0], wide),
        occ_energy_i,
        occ_energy_j,
        virt_energy.reshape(1, wide),
        vv_mask,
        pair_domain,
        vv_factors,
    )


def solution(mesh):
    placed = (
        P("pair", "integ", "virt", None),
        P("integ", None, None),
        P(None, "integ", None),
        P("pair"),
        P("integ"),
        P(),
        P(),
        P("pair", "integ", None),
    )
    return jax.shard_map(
        functools.partial(body, mesh.shape["virt"], mesh.shape["integ"]),
        mesh=mesh,
        in_specs=placed,
        out_specs=P("pair", "integ", "virt", None),
        check_vma=False,
    )
```

time: 68.8 us -> 31.4 us (0.46)
  blocking collectives: 44.2 us -> 0 us
  Pallas kernels: 0 us -> 23.7 us
  between operations: 14.8 us -> 1.32 us
  local copies, waits for them, and re-layouts: 0.8 us -> 5.73 us
  matrix products: 4.6 us -> 0 us
  other arithmetic: 3.96 us -> 0 us
    all_gather x2 -> x0, blocking collectives: 26 us -> none  [the longest x1 16.1 us: body(): all_pairs = lax.all_gather(full_rows, 'integ', axis=1, tiled=True)[0]]
    pallas_call x0 -> x1, Pallas kernels: none -> 23.7 us  [body(): pl.pallas_call(functools.partial(kernel, columns, planes), out_shape=jax....]
    psum x1 -> x0, blocking collectives: 18.2 us -> none  [body(): zeta = lax.psum(partial_zeta, 'integ')]
    unnamed x8 -> x13, local copies, waits for them, and re-layouts: 0.13 us -> 5.73 us
    dot_general x4 -> x0, matrix products: 4.6 us -> none  [the longest x1 2.77 us: body(): jnp.einsum('jqad,qbd->jab', weighted, factors, preferred_element_type=jnp...]
    convert_element_type x3 -> x0, other arithmetic: 2.18 us -> none  [the longest x1 0.83 us: body(): (amplitudes[0, 0].astype(jnp.float32) * domain_rows[:, None] * domain[Non...]
    mul x1 -> x0, other arithmetic: 1.78 us -> none  [body(): factors = vv_factors * grid[None]]
  transfers between devices with their start and end apart: 1 -> 0, of which waited for: 0 -> 0; matrix products, arithmetic and copies ran while one was open for 1% -> 0% of each run, Pallas kernels for 0% -> 0%
where the time goes in v1:
time: 31.4 us; the launch traced here: 30.8 us
  Pallas kernels  23.7 us (75%)
  local copies, waits for them, and re-layouts  5.73 us (18%)
  between operations  1.32 us (4%)
    pallas_call x1, Pallas kernels, body(): pl.pallas_call(functools.partial(kernel, columns, planes), out_shape=jax....  23.7 us
    unnamed x13, local copies, waits for them, and re-layouts  5.73 us

profile of v1, /device:TPU:0, one launch (start us, length us, event | category | flops | bytes accessed | tf_op | source)
XLA Modules:
  0.0 30.8 jit_solution(18302739148841268041)
XLA Ops:
  1.3 0.0 copy-start
  1.3 1.6 %copy-done = bf16[16,256,256]{2,1,0:T(8,128)(2,1)S(1)} copy-done((bf16[16,256,256]{2,1,0:T(8,128)(2,1)S(1)}, bf16[16,256,256]{2,1,0:T(8,128)(2,1)}, u32[]{:S(2)}) %copy-start) | copy-done | bytes 2097176
  2.9 0.0 copy-start.1
  2.9 0.8 %copy-done.1 = bf16[1,1,64,256]{3,2,1,0:T(8,128)(2,1)S(1)} copy-done((bf16[1,1,64,256]{3,2,1,0:T(8,128)(2,1)S(1)}, bf16[1,1,64,256]{3,2,1,0:T(8,128)(2,1)}, u32[]{:S(2)}) %copy-start.1) | copy-done | bytes 32792
  3.6 0.0 copy-start.2
  3.6 0.8 %copy-done.2 = bf16[64,1,256]{2,0,1:T(8,128)(2,1)S(1)} copy-done((bf16[64,1,256]{2,0,1:T(8,128)(2,1)S(1)}, bf16[64,1,256]{2,0,1:T(8,128)(2,1)}, u32[]{:S(2)}) %copy-start.2) | copy-done | bytes 32792
  4.4 0.0 copy-start.3
  4.4 0.7 %copy-done.3 = f32[256]{0:T(256)S(1)} copy-done((f32[256]{0:T(256)S(1)}, f32[256]{0:T(256)}, u32[]{:S(2)}) %copy-start.3) | copy-done | bytes 1048
  5.1 0.0 copy-start.4
  5.1 0.7 %copy-done.4 = s32[2,2]{1,0:T(2,128)S(1)} copy-done((s32[2,2]{1,0:T(2,128)S(1)}, s32[2,2]{1,0:T(2,128)}, u32[]{:S(2)}) %copy-start.4) | copy-done | bytes 40
  5.8 0.0 copy-start.5
  5.8 0.7 %copy-done.5 = s32[1,1,2]{2,1,0:T(1,128)S(1)} copy-done((s32[1,1,2]{2,1,0:T(1,128)S(1)}, s32[1,1,2]{2,1,0:T(1,128)}, u32[]{:S(2)}) %copy-start.5) | copy-done | bytes 32
  6.4 23.7 %shard_map.82 = bf16[1,1,64,256]{3,2,1,0:T(8,128)(2,1)S(1)} custom-call(bf16[1,1,64,256]{3,2,1,0:T(8,128)(2,1)S(1)} %copy-done.1, bf16[64,256]{1,0:T(8,128)(2,1)S(1)} %bitcast.2, f32[1]{0:T(128)S(6)} %copy.10.occ_i_ref, f32[1]{0:T(128)S(6)} %copy.11.occ_j_ref, f32[1,256]{1,0:T(1,128)S(1)} %bitcast.3, s32[2,2]{1,0:T(2,128)S(1)} %copy-done.4, ...), custom_call_target="tpu_custom_call" | custom-call | flops 1073741824 | bytes 2097152 | tf_op jit(solution)/shard_map/pallas_call | solution.py:352
  30.2 0.6 %copy.12 = bf16[1,1,64,256]{3,2,1,0:T(8,128)(2,1)} copy(bf16[1,1,64,256]{3,2,1,0:T(8,128)(2,1)S(1)} %shard_map.82) | data formatting | bytes 65536
Async XLA Ops:
  1.3 1.6 %copy-start = (bf16[16,256,256]{2,1,0:T(8,128)(2,1)S(1)}, bf16[16,256,256]{2,1,0:T(8,128)(2,1)}, u32[]{:S(2)}) copy-start(bf16[16,256,256]{2,1,0:T(8,128)(2,1)} %vv_ref.1) | copy-start | bytes 6291460
  2.9 0.8 %copy-start.1 = (bf16[1,1,64,256]{3,2,1,0:T(8,128)(2,1)S(1)}, bf16[1,1,64,256]{3,2,1,0:T(8,128)(2,1)}, u32[]{:S(2)}) copy-start(bf16[1,1,64,256]{3,2,1,0:T(8,128)(2,1)} %amp_ref.1) | copy-start | bytes 98308
  3.6 0.8 %copy-start.2 = (bf16[64,1,256]{2,0,1:T(8,128)(2,1)S(1)}, bf16[64,1,256]{2,0,1:T(8,128)(2,1)}, u32[]{:S(2)}) copy-start(bf16[64,1,256]{2,0,1:T(8,128)(2,1)} %param.10) | copy-start | bytes 98308
  4.4 0.7 %copy-start.3 = (f32[256]{0:T(256)S(1)}, f32[256]{0:T(256)}, u32[]{:S(2)}) copy-start(f32[256]{0:T(256)} %param.13) | copy-start | bytes 3076
  5.1 0.7 %copy-start.4 = (s32[2,2]{1,0:T(2,128)S(1)}, s32[2,2]{1,0:T(2,128)}, u32[]{:S(2)}) copy-start(s32[2,2]{1,0:T(2,128)} %vv_mask_ref.1) | copy-start | bytes 52
  5.8 0.7 %copy-start.5 = (s32[1,1,2]{2,1,0:T(1,128)S(1)}, s32[1,1,2]{2,1,0:T(1,128)}, u32[]{:S(2)}) copy-start(s32[1,1,2]{2,1,0:T(1,128)} %domain_ref.1) | copy-start | bytes 28

commit v2 on v1

--- a/solution.py
+++ b/solution.py
@@ -32,6 +32,15 @@
 def kernel(
     columns,
     planes,
+    amp_hbm,
+    ov_hbm,
+    occ_i_hbm,
+    occ_j_hbm,
+    energy_hbm,
+    vv_mask_hbm,
+    domain_hbm,
+    vv_hbm,
+    out_ref,
     amp_ref,
     ov_ref,
     occ_i_ref,
@@ -39,14 +48,13 @@
     energy_ref,
     vv_mask_ref,
     domain_ref,
-    vv_ref,
-    out_ref,
     factors,
     lines,
     pairs,
     ov_mine,
     zetas,
     terms,
+    hops,
     parts,
     load_sem,
     line_send,
@@ -57,6 +65,8 @@
     ov_recv,
     zeta_send,
     zeta_recv,
+    hop_send,
+    hop_recv,
     part_send,
     part_recv,
 ):
@@ -64,7 +74,7 @@
     virt = lax.axis_index("virt")
     integ = lax.axis_index("integ")
     share, wide = amp_ref.shape[2], amp_ref.shape[3]
-    aux = vv_ref.shape[0]
+    aux = factors.shape[0]
     tiles = wide // TILE_SIZE
     held = planes // columns
     home = integ // held
@@ -83,8 +93,23 @@
     def rows(which):
         return pl.ds(pl.multiple_of(which * share, share), share)
 
-    load = pltpu.make_async_copy(vv_ref, factors, load_sem)
-    load.start()
+    loads = [
+        pltpu.make_async_copy(src, dst, load_sem.at[which])
+        for which, (src, dst) in enumerate(
+            (
+                (amp_hbm, amp_ref),
+                (domain_hbm, domain_ref),
+                (ov_hbm, ov_ref),
+                (vv_mask_hbm, vv_mask_ref),
+                (energy_hbm, energy_ref),
+                (occ_i_hbm, occ_i_ref),
+                (occ_j_hbm, occ_j_ref),
+                (vv_hbm, factors),
+            )
+        )
+    ]
+    for load in loads:
+        load.start()
 
     barrier = pltpu.get_barrier_semaphore()
 
@@ -98,10 +123,8 @@
     for step in range(1, columns):
         greet(lax.rem(virt + step, columns), integ)
 
-    @pl.when(home != virt)
-    def _():
-        for step in range(1, planes):
-            greet(home, lax.rem(integ + step, planes))
+    loads[0].wait()
+    loads[1].wait()
 
     domain = [domain_ref[0, 0, tile].astype(F32) for tile in range(tiles)]
     row_index = virt * share + lax.broadcasted_iota(jnp.int32, (share, wide), 0)
@@ -109,8 +132,7 @@
     pair_mask = over_tiles(row_index, domain) * over_tiles(col_index, domain)
     lines[integ] = (amp_ref[0, 0].astype(F32) * pair_mask).astype(BF16)
 
-    own_home = jnp.where(home == virt, 1, 0)
-    pl.semaphore_wait(barrier, planes - 1 + (columns - 1) * (held + 1 - own_home))
+    pl.semaphore_wait(barrier, planes + columns - 2)
 
     def line_copy(step):
         return remote(
@@ -155,12 +177,16 @@
     for step in range(1, planes):
         line_copy(step).start()
     forward(integ)
+    loads[2].wait()
 
     @pl.when(home == virt)
     def _():
         for step in range(1, planes):
             ov_copy(step).start()
         ov_mine[slot] = ov_ref[pl.ds(pl.multiple_of(integ * aux, aux), aux)]
+
+    for load in loads[3:7]:
+        load.wait()
 
     row_in = lax.broadcasted_iota(jnp.int32, (wide, wide), 0) // TILE_SIZE
     col_in = lax.broadcasted_iota(jnp.int32, (wide, wide), 1) // TILE_SIZE
@@ -174,7 +200,7 @@
     energy_rows = jnp.sum(jnp.where(col_index == row_index, energy, 0.0), axis=1, keepdims=True)
     denom = energy_rows + energy - occ_i_ref[0] - occ_j_ref[0]
     scale = pair_mask / denom
-    load.wait()
+    loads[7].wait()
 
     @pl.loop(0, aux)
     def _(q):
@@ -256,27 +282,42 @@
         upper = zeta.astype(BF16)
         return upper, (zeta - upper.astype(F32)).astype(BF16)
 
-    def part_copy(first, row):
-        return remote(
-            terms.at[first, pl.ds(row * share, share)],
+    def hop_copy(first, step):
+        row = lax.rem(virt + step, columns)
+        return remote(
+            terms.at[first, rows(row)],
+            hops.at[virt * held + first],
+            hop_send.at[first * columns + step],
+            hop_recv.at[virt * held + first],
+            row,
+            integ,
+        )
+
+    def part_copy(which):
+        return remote(
+            hops.at[which],
             parts.at[integ],
-            part_send.at[first * columns + row],
+            part_send.at[which],
             part_recv.at[integ],
-            row,
-            virt * held + first,
-        )
+            virt,
+            which,
+        )
+
+    def pass_on(which):
+        @pl.when(which != integ)
+        def _():
+            part_copy(which).start()
+
+        @pl.when(which == integ)
+        def _():
+            parts[integ] = hops[which]
 
     def hand_over(first):
-        for row in range(columns):
-            mine = jnp.logical_and(virt == row, virt * held + first == integ)
-
-            @pl.when(jnp.logical_not(mine))
-            def _(row=row):
-                part_copy(first, row).start()
-
-            @pl.when(mine)
-            def _(row=row):
-                parts[integ] = terms[first, pl.ds(row * share, share)]
+        for step in range(1, columns):
+            hop_copy(first, step).start()
+        which = virt * held + first
+        hops[which] = terms[first, rows(virt)]
+        pass_on(which)
 
     if held == 1:
         total = ladder(0)
@@ -291,17 +332,22 @@
             terms[first] = (ladder(first) + cycle(first, upper, lower)).astype(BF16)
             hand_over(first)
 
-    for source in range(planes):
-        @pl.when(jnp.logical_or(home != virt, integ != source))
-        def _(source=source):
+    for step in range(1, columns):
+        source = lax.rem(virt + step, columns)
+        for first in range(held):
+            which = source * held + first
+            landed = hops.at[which]
             remote(
-                parts.at[source],
-                parts.at[source],
-                part_send.at[0],
-                part_recv.at[source],
-                home,
-                integ,
+                landed, landed, hop_send.at[0], hop_recv.at[which], source, integ
             ).wait_recv()
+            pass_on(which)
+
+    for step in range(1, planes):
+        source = lax.rem(integ + step, planes)
+        landed = parts.at[source]
+        remote(
+            landed, landed, part_send.at[0], part_recv.at[source], virt, source
+        ).wait_recv()
 
     total = parts[0].astype(F32)
     for source in range(1, planes):
@@ -323,12 +369,10 @@
             ov_copy(step).wait_send()
 
     for first in range(held):
-        for row in range(columns):
-            mine = jnp.logical_and(virt == row, virt * held + first == integ)
-
-            @pl.when(jnp.logical_not(mine))
-            def _(first=first, row=row):
-                part_copy(first, row).wait_send()
+        for step in range(1, columns):
+            hop_copy(first, step).wait_send()
+    for step in range(1, planes):
+        part_copy(lax.rem(integ + step, planes)).wait_send()
 
 
 def body(
@@ -347,14 +391,21 @@
     aux = vv_factors.shape[0]
     held = planes // columns
     vmem = pl.BlockSpec(memory_space=pltpu.VMEM)
-    smem = pl.BlockSpec(memory_space=pltpu.SMEM)
+    smem = pltpu.SMEM
     dma = pltpu.SemaphoreType.DMA
     return pl.pallas_call(
         functools.partial(kernel, columns, planes),
         out_shape=jax.ShapeDtypeStruct(amplitudes.shape, BF16),
-        in_specs=[vmem, vmem, smem, smem, vmem, smem, smem, pl.BlockSpec(memory_space=pl.ANY)],
+        in_specs=[pl.BlockSpec(memory_space=pltpu.HBM)] * 8,
         out_specs=vmem,
         scratch_shapes=[
+            pltpu.VMEM(amplitudes.shape, BF16),
+            pltpu.VMEM((ov_factors.shape[0], wide), BF16),
+            smem(occ_energy_i.shape, F32),
+            smem(occ_energy_j.shape, F32),
+            pltpu.VMEM((1, wide), F32),
+            smem(vv_mask.shape, jnp.int32),
+            smem(pair_domain.shape, jnp.int32),
             pltpu.VMEM((aux, wide, wide), BF16),
             pltpu.VMEM((planes, share, wide), BF16),
             pltpu.VMEM((held, wide, wide), BF16),
@@ -362,7 +413,8 @@
             pltpu.VMEM((columns, aux, wide), F32),
             pltpu.VMEM((held, wide, wide), BF16),
             pltpu.VMEM((planes, share, wide), BF16),
-            dma,
+            pltpu.VMEM((planes, share, wide), BF16),
+            dma((8,)),
             dma((planes,)),
             dma((planes,)),
             dma((planes,)),
@@ -373,9 +425,11 @@
             dma((columns,)),
             dma((planes,)),
             dma((planes,)),
+            dma((planes,)),
+            dma((planes,)),
         ],
         compiler_params=pltpu.CompilerParams(
-            collective_id=0, has_side_effects=True, vmem_limit_bytes=40 * 1024 * 1024
+            collective_id=0, has_side_effects=True, vmem_limit_bytes=60 * 1024 * 1024
         ),
         cost_estimate=pl.CostEstimate(
             flops=4 * held * aux * wide**3, bytes_accessed=2 * aux * wide * wide, transcendentals=0

time: 31.4 us -> 27.7 us (0.88)
  the two profiles are of different devices: /device:TPU:0 before, /device:TPU:2 now
where the time goes in v2:
time: 27.7 us; the launch traced here: 27.5 us
  Pallas kernels  24.8 us (90%)
  local copies, waits for them, and re-layouts  1.38 us (5%)
  between operations  1.3 us (5%)
    pallas_call x1, Pallas kernels, body(): pl.pallas_call(functools.partial(kernel, columns, planes), out_shape=jax....  24.8 us
    unnamed x1, local copies, waits for them, and re-layouts  1.38 us

profile of v2, /device:TPU:2, one launch (start us, length us, event | category | flops | bytes accessed | tf_op | source)
XLA Modules:
  0.0 27.5 jit_solution(11541829320376678357)
XLA Ops:
  1.3 24.8 %shard_map.82 = bf16[1,1,64,256]{3,2,1,0:T(8,128)(2,1)} custom-call(bf16[1,1,64,256]{3,2,1,0:T(8,128)(2,1)} %amp_hbm.1, bf16[64,256]{1,0:T(8,128)(2,1)} %bitcast.2, f32[1]{0:T(128)S(6)} %copy.10.occ_i_hbm, f32[1]{0:T(128)S(6)} %copy.11.occ_j_hbm, f32[1,256]{1,0:T(1,128)} %bitcast.3, s32[2,2]{1,0:T(2,128)} %vv_mask_hbm.1, s32[1,1,2]{2,1,0:T(1,128)} %domain_hbm.1, ...), custom_call_target="tpu_custom_call" | custom-call | flops 1073741824 | bytes 2097152 | tf_op jit(solution)/shard_map/pallas_call | solution.py:396
  26.1 1.4 %copy.12 = bf16[1,1,64,256]{3,2,1,0:T(8,128)(2,1)} copy(bf16[1,1,64,256]{3,2,1,0:T(8,128)(2,1)} %shard_map.82) | data formatting | bytes 65536

commit v3 on v2

--- a/solution.py
+++ b/solution.py
@@ -8,7 +8,8 @@
 from jax.sharding import PartitionSpec as P
 
 TILE_SIZE = 128
-GROUP = 4
+GROUP = 8
+HALVES = 2
 MESH = pl.DeviceIdType.MESH
 F32 = jnp.float32
 BF16 = jnp.bfloat16
@@ -49,16 +50,15 @@
     vv_mask_ref,
     domain_ref,
     factors,
-    lines,
+    line,
     pairs,
     ov_mine,
     zetas,
+    zeta_rows,
     terms,
     hops,
     parts,
     load_sem,
-    line_send,
-    line_recv,
     pair_send,
     pair_recv,
     ov_send,
@@ -122,6 +122,11 @@
         greet(virt, lax.rem(integ + step, planes))
     for step in range(1, columns):
         greet(lax.rem(virt + step, columns), integ)
+    for first in range(held):
+        @pl.when(virt * held + first != integ)
+        def _(first=first):
+            for step in range(1, columns):
+                greet(lax.rem(virt + step, columns), virt * held + first)
 
     loads[0].wait()
     loads[1].wait()
@@ -130,19 +135,10 @@
     row_index = virt * share + lax.broadcasted_iota(jnp.int32, (share, wide), 0)
     col_index = lax.broadcasted_iota(jnp.int32, (share, wide), 1)
     pair_mask = over_tiles(row_index, domain) * over_tiles(col_index, domain)
-    lines[integ] = (amp_ref[0, 0].astype(F32) * pair_mask).astype(BF16)
-
-    pl.semaphore_wait(barrier, planes + columns - 2)
-
-    def line_copy(step):
-        return remote(
-            lines.at[integ],
-            lines.at[integ],
-            line_send.at[step],
-            line_recv.at[integ],
-            virt,
-            lax.rem(integ + step, planes),
-        )
+    line[...] = (amp_ref[0, 0].astype(F32) * pair_mask).astype(BF16)
+
+    away = jnp.where(home != virt, planes - 1, 0)
+    pl.semaphore_wait(barrier, planes + columns - 2 + away)
 
     def ov_copy(step):
         to_integ = lax.rem(integ + step, planes)
@@ -155,28 +151,27 @@
             to_integ,
         )
 
-    def pair_copy(which):
+    def pair_copy(to_integ):
         return remote(
-            lines.at[which],
-            pairs.at[which % held, rows(virt)],
-            pair_send.at[which],
-            pair_recv.at[(which % held) * columns + virt],
-            which // held,
-            integ,
-        )
-
-    def forward(which):
-        @pl.when(which // held != virt)
-        def _():
-            pair_copy(which).start()
-
-        @pl.when(which // held == virt)
-        def _():
-            pairs[which % held, rows(virt)] = lines[which]
-
-    for step in range(1, planes):
-        line_copy(step).start()
-    forward(integ)
+            line,
+            pairs.at[slot, rows(virt)],
+            pair_send.at[to_integ],
+            pair_recv.at[slot * columns + virt],
+            home,
+            to_integ,
+        )
+
+    for turn in range(planes):
+        to_integ = jnp.where(2 * integ < planes, planes - 1 - turn, turn)
+
+        @pl.when(jnp.logical_or(home != virt, to_integ != integ))
+        def _(to_integ=to_integ):
+            pair_copy(to_integ).start()
+
+    @pl.when(home == virt)
+    def _():
+        pairs[slot, rows(virt)] = line[...]
+
     loads[2].wait()
 
     @pl.when(home == virt)
@@ -206,33 +201,26 @@
     def _(q):
         factors[q] = factors[q] * grid
 
-    for step in range(1, planes):
-        which = lax.rem(integ + step, planes)
-        line_copy_in = remote(
-            lines.at[which], lines.at[which], line_send.at[step], line_recv.at[which], virt, which
-        )
-        line_copy_in.wait_recv()
-        forward(which)
-
     for first in range(held):
-        @pl.when(jnp.logical_or(home != virt, slot != first))
+        @pl.when(virt * held + first != integ)
         def _(first=first):
             ov_in = remote(
                 ov_mine.at[first], ov_mine.at[first], ov_send.at[0], ov_recv.at[first], virt, integ
             )
             ov_in.wait_recv()
 
-        for step in range(1, columns):
-            source = lax.rem(virt + step, columns)
-            landed = pairs.at[first, rows(source)]
-            remote(
-                landed,
-                landed,
-                pair_send.at[0],
-                pair_recv.at[first * columns + source],
-                source,
-                integ,
-            ).wait_recv()
+        for source in range(columns):
+            @pl.when(jnp.logical_or(virt * held + first != integ, source != virt))
+            def _(first=first, source=source):
+                landed = pairs.at[first, rows(source)]
+                remote(
+                    landed,
+                    landed,
+                    pair_send.at[0],
+                    pair_recv.at[first * columns + source],
+                    virt,
+                    integ,
+                ).wait_recv()
 
     zeta_part = jnp.zeros((aux, wide), F32)
     for first in range(held):
@@ -253,22 +241,31 @@
     for step in range(1, columns):
         zeta_copy(step).start()
 
-    def ladder(first):
+    depth = wide // HALVES
+    near = columns // HALVES
+    my_half = virt // near
+
+    def lines_of(half):
+        return pl.ds(pl.multiple_of(half * depth, depth), depth)
+
+    def ladder(first, half):
         amps = pairs[first]
 
         def add(group, total):
             block = factors[pl.ds(group * GROUP, GROUP)]
-            weighted = dot_nn(block.reshape(GROUP * wide, wide), amps).astype(BF16)
+            some = factors[pl.ds(group * GROUP, GROUP), lines_of(half)]
+            weighted = dot_nn(some.reshape(GROUP * depth, wide), amps).astype(BF16)
             for q in range(GROUP):
-                total = total + dot_nt(weighted[q * wide:(q + 1) * wide], block[q])
+                total = total + dot_nt(weighted[q * depth:(q + 1) * depth], block[q])
             return total
 
-        return lax.fori_loop(0, aux // GROUP, add, jnp.zeros((wide, wide), F32))
-
-    def cycle(first, upper, lower):
+        return lax.fori_loop(0, aux // GROUP, add, jnp.zeros((depth, wide), F32))
+
+    def cycle(first, half):
+        upper, lower = zeta_rows[0, lines_of(half)], zeta_rows[1, lines_of(half)]
         return dot_nn(upper, ov_mine[first]) + dot_nn(lower, ov_mine[first])
 
-    def zeta_halves():
+    def gather_zeta():
         for step in range(1, columns):
             source = lax.rem(virt + step, columns)
             landed = zetas.at[source]
@@ -280,14 +277,14 @@
             zeta = zeta + zetas[column]
         zeta = zeta.T
         upper = zeta.astype(BF16)
-        return upper, (zeta - upper.astype(F32)).astype(BF16)
-
-    def hop_copy(first, step):
-        row = lax.rem(virt + step, columns)
+        zeta_rows[0] = upper
+        zeta_rows[1] = (zeta - upper.astype(F32)).astype(BF16)
+
+    def hop_copy(first, row):
         return remote(
             terms.at[first, rows(row)],
             hops.at[virt * held + first],
-            hop_send.at[first * columns + step],
+            hop_send.at[first * columns + row],
             hop_recv.at[virt * held + first],
             row,
             integ,
@@ -312,35 +309,48 @@
         def _():
             parts[integ] = hops[which]
 
-    def hand_over(first):
-        for step in range(1, columns):
-            hop_copy(first, step).start()
-        which = virt * held + first
-        hops[which] = terms[first, rows(virt)]
-        pass_on(which)
+    def hand_over(first, half):
+        for step in range(near):
+            row = half * near + lax.rem(virt + 1 + step, near)
+
+            @pl.when(row != virt)
+            def _(row=row):
+                hop_copy(first, row).start()
+
+            @pl.when(row == virt)
+            def _(row=row):
+                hops[virt * held + first] = terms[first, rows(row)]
+                pass_on(virt * held + first)
+
+    def work(first):
+        for turn in range(HALVES):
+            half = lax.rem(my_half + 1 + turn, HALVES)
+            total = ladder(first, half)
+            if held == 1 and turn == 0:
+                gather_zeta()
+            terms[first, lines_of(half)] = (total + cycle(first, half)).astype(BF16)
+            hand_over(first, half)
 
     if held == 1:
-        total = ladder(0)
-        upper, lower = zeta_halves()
-        terms[0] = (total + cycle(0, upper, lower)).astype(BF16)
-        hand_over(0)
+        work(0)
     else:
-        upper, lower = zeta_halves()
-
-        @pl.loop(0, held)
-        def _(first):
-            terms[first] = (ladder(first) + cycle(first, upper, lower)).astype(BF16)
-            hand_over(first)
-
-    for step in range(1, columns):
-        source = lax.rem(virt + step, columns)
-        for first in range(held):
-            which = source * held + first
-            landed = hops.at[which]
-            remote(
-                landed, landed, hop_send.at[0], hop_recv.at[which], source, integ
-            ).wait_recv()
-            pass_on(which)
+        gather_zeta()
+        pl.loop(0, held)(work)
+
+    for turn in range(HALVES):
+        half = lax.rem(my_half + 1 + turn, HALVES)
+        for step in range(near):
+            source = half * near + lax.rem(virt + 1 + step, near)
+
+            @pl.when(source != virt)
+            def _(source=source):
+                for first in range(held):
+                    which = source * held + first
+                    landed = hops.at[which]
+                    remote(
+                        landed, landed, hop_send.at[0], hop_recv.at[which], source, integ
+                    ).wait_recv()
+                    pass_on(which)
 
     for step in range(1, planes):
         source = lax.rem(integ + step, planes)
@@ -354,14 +364,12 @@
         total = total + parts[source].astype(F32)
     out_ref[0, 0] = (total * scale).astype(BF16)
 
-    for step in range(1, planes):
-        line_copy(step).wait_send()
     for step in range(1, columns):
         zeta_copy(step).wait_send()
-    for which in range(planes):
-        @pl.when(which // held != virt)
-        def _(which=which):
-            pair_copy(which).wait_send()
+    for to_integ in range(planes):
+        @pl.when(jnp.logical_or(home != virt, to_integ != integ))
+        def _(to_integ=to_integ):
+            pair_copy(to_integ).wait_send()
 
     @pl.when(home == virt)
     def _():
@@ -370,7 +378,7 @@
 
     for first in range(held):
         for step in range(1, columns):
-            hop_copy(first, step).wait_send()
+            hop_copy(first, lax.rem(virt + step, columns)).wait_send()
     for step in range(1, planes):
         part_copy(lax.rem(integ + step, planes)).wait_send()
 
@@ -407,16 +415,15 @@
             smem(vv_mask.shape, jnp.int32),
             smem(pair_domain.shape, jnp.int32),
             pltpu.VMEM((aux, wide, wide), BF16),
-            pltpu.VMEM((planes, share, wide), BF16),
+            pltpu.VMEM((share, wide), BF16),
             pltpu.VMEM((held, wide, wide), BF16),
             pltpu.VMEM((held, aux, wide), BF16),
             pltpu.VMEM((columns, aux, wide), F32),
+            pltpu.VMEM((2, wide, aux), BF16),
             pltpu.VMEM((held, wide, wide), BF16),
             pltpu.VMEM((planes, share, wide), BF16),
             pltpu.VMEM((planes, share, wide), BF16),
             dma((8,)),
-            dma((planes,)),
-            dma((planes,)),
             dma((planes,)),
             dma((planes,)),
             dma((planes,)),

time: 27.7 us -> 25.3 us (0.913)
  the two profiles are of different devices: /device:TPU:2 before, /device:TPU:0 now
where the time goes in v3:
time: 25.3 us; the launch traced here: 24.8 us
  Pallas kernels  22.1 us (87%)
  local copies, waits for them, and re-layouts  1.38 us (5%)
  between operations  1.3 us (5%)
    pallas_call x1, Pallas kernels, body(): pl.pallas_call(functools.partial(kernel, columns, planes), out_shape=jax....  22.1 us
    unnamed x1, local copies, waits for them, and re-layouts  1.38 us

profile of v3, /device:TPU:0, one launch (start us, length us, event | category | flops | bytes accessed | tf_op | source)
XLA Modules:
  0.0 24.8 jit_solution(13685195297588136067)
XLA Ops:
  1.3 22.1 %shard_map.82 = bf16[1,1,64,256]{3,2,1,0:T(8,128)(2,1)} custom-call(bf16[1,1,64,256]{3,2,1,0:T(8,128)(2,1)} %amp_hbm.1, bf16[64,256]{1,0:T(8,128)(2,1)} %bitcast.2, f32[1]{0:T(128)S(6)} %copy.10.occ_i_hbm, f32[1]{0:T(128)S(6)} %copy.11.occ_j_hbm, f32[1,256]{1,0:T(1,128)} %bitcast.3, s32[2,2]{1,0:T(2,128)} %vv_mask_hbm.1, s32[1,1,2]{2,1,0:T(1,128)} %domain_hbm.1, ...), custom_call_target="tpu_custom_call" | custom-call | flops 1073741824 | bytes 2097152 | tf_op jit(solution)/shard_map/pallas_call | solution.py:404
  23.4 1.4 %copy.12 = bf16[1,1,64,256]{3,2,1,0:T(8,128)(2,1)} copy(bf16[1,1,64,256]{3,2,1,0:T(8,128)(2,1)} %shard_map.82) | data formatting | bytes 65536

commit v4 on v3

--- a/solution.py
+++ b/solution.py
@@ -42,7 +42,6 @@
     domain_hbm,
     vv_hbm,
     out_ref,
-    amp_ref,
     ov_ref,
     occ_i_ref,
     occ_j_ref,
@@ -50,7 +49,7 @@
     vv_mask_ref,
     domain_ref,
     factors,
-    line,
+    domains,
     pairs,
     ov_mine,
     zetas,
@@ -63,6 +62,8 @@
     pair_recv,
     ov_send,
     ov_recv,
+    domain_send,
+    domain_recv,
     zeta_send,
     zeta_recv,
     hop_send,
@@ -73,7 +74,7 @@
     pair = lax.axis_index("pair")
     virt = lax.axis_index("virt")
     integ = lax.axis_index("integ")
-    share, wide = amp_ref.shape[2], amp_ref.shape[3]
+    share, wide = amp_hbm.shape[2], amp_hbm.shape[3]
     aux = factors.shape[0]
     tiles = wide // TILE_SIZE
     held = planes // columns
@@ -97,7 +98,7 @@
         pltpu.make_async_copy(src, dst, load_sem.at[which])
         for which, (src, dst) in enumerate(
             (
-                (amp_hbm, amp_ref),
+                (amp_hbm.at[0, 0], pairs.at[slot, rows(virt)]),
                 (domain_hbm, domain_ref),
                 (ov_hbm, ov_ref),
                 (vv_mask_hbm, vv_mask_ref),
@@ -108,8 +109,12 @@
             )
         )
     ]
-    for load in loads:
+    for load in loads[1:]:
         load.start()
+
+    @pl.when(home == virt)
+    def _():
+        loads[0].start()
 
     barrier = pltpu.get_barrier_semaphore()
 
@@ -128,15 +133,6 @@
             for step in range(1, columns):
                 greet(lax.rem(virt + step, columns), virt * held + first)
 
-    loads[0].wait()
-    loads[1].wait()
-
-    domain = [domain_ref[0, 0, tile].astype(F32) for tile in range(tiles)]
-    row_index = virt * share + lax.broadcasted_iota(jnp.int32, (share, wide), 0)
-    col_index = lax.broadcasted_iota(jnp.int32, (share, wide), 1)
-    pair_mask = over_tiles(row_index, domain) * over_tiles(col_index, domain)
-    line[...] = (amp_ref[0, 0].astype(F32) * pair_mask).astype(BF16)
-
     away = jnp.where(home != virt, planes - 1, 0)
     pl.semaphore_wait(barrier, planes + columns - 2 + away)
 
@@ -153,7 +149,7 @@
 
     def pair_copy(to_integ):
         return remote(
-            line,
+            amp_hbm.at[0, 0],
             pairs.at[slot, rows(virt)],
             pair_send.at[to_integ],
             pair_recv.at[slot * columns + virt],
@@ -168,15 +164,28 @@
         def _(to_integ=to_integ):
             pair_copy(to_integ).start()
 
+    loads[1].wait()
+    domain = [domain_ref[0, 0, tile].astype(F32) for tile in range(tiles)]
+    loads[2].wait()
+
+    def domain_copy(step):
+        return remote(
+            domains.at[slot],
+            domains.at[slot],
+            domain_send.at[step],
+            domain_recv.at[slot],
+            virt,
+            lax.rem(integ + step, planes),
+        )
+
     @pl.when(home == virt)
     def _():
-        pairs[slot, rows(virt)] = line[...]
-
-    loads[2].wait()
-
-    @pl.when(home == virt)
-    def _():
+        for tile in range(tiles):
+            domains[slot, :, pl.ds(tile * TILE_SIZE, TILE_SIZE)] = jnp.full(
+                (domains.shape[1], TILE_SIZE), domain[tile], F32
+            )
         for step in range(1, planes):
+            domain_copy(step).start()
             ov_copy(step).start()
         ov_mine[slot] = ov_ref[pl.ds(pl.multiple_of(integ * aux, aux), aux)]
 
@@ -191,6 +200,9 @@
             here = jnp.logical_and(row_in == first, col_in == second)
             grid = jnp.where(here, vv_mask_ref[first, second].astype(F32), grid)
     grid = grid.astype(BF16)
+    row_index = virt * share + lax.broadcasted_iota(jnp.int32, (share, wide), 0)
+    col_index = lax.broadcasted_iota(jnp.int32, (share, wide), 1)
+    pair_mask = over_tiles(row_index, domain) * over_tiles(col_index, domain)
     energy = jnp.broadcast_to(energy_ref[...], (share, wide))
     energy_rows = jnp.sum(jnp.where(col_index == row_index, energy, 0.0), axis=1, keepdims=True)
     denom = energy_rows + energy - occ_i_ref[0] - occ_j_ref[0]
@@ -208,6 +220,14 @@
                 ov_mine.at[first], ov_mine.at[first], ov_send.at[0], ov_recv.at[first], virt, integ
             )
             ov_in.wait_recv()
+            remote(
+                domains.at[first],
+                domains.at[first],
+                domain_send.at[0],
+                domain_recv.at[first],
+                virt,
+                integ,
+            ).wait_recv()
 
         for source in range(columns):
             @pl.when(jnp.logical_or(virt * held + first != integ, source != virt))
@@ -222,6 +242,24 @@
                     integ,
                 ).wait_recv()
 
+    @pl.when(home == virt)
+    def _():
+        loads[0].wait()
+
+    for first in range(held):
+        for upper in range(tiles):
+            for lower in range(tiles):
+                spot = (
+                    first,
+                    pl.ds(upper * TILE_SIZE, TILE_SIZE),
+                    pl.ds(lower * TILE_SIZE, TILE_SIZE),
+                )
+                kept = (
+                    domains[first, 0:1, pl.ds(upper * TILE_SIZE, TILE_SIZE)]
+                    * domains[first, 0:1, pl.ds(lower * TILE_SIZE, TILE_SIZE)]
+                ).astype(BF16)
+                pairs[spot] = pairs[spot] * kept
+
     zeta_part = jnp.zeros((aux, wide), F32)
     for first in range(held):
         amps = pairs[first]
@@ -241,19 +279,16 @@
     for step in range(1, columns):
         zeta_copy(step).start()
 
-    depth = wide // HALVES
     near = columns // HALVES
     my_half = virt // near
 
-    def lines_of(half):
-        return pl.ds(pl.multiple_of(half * depth, depth), depth)
-
-    def ladder(first, half):
+    def ladder(first, start, depth):
         amps = pairs[first]
+        chosen = pl.ds(pl.multiple_of(start, share), depth)
 
         def add(group, total):
             block = factors[pl.ds(group * GROUP, GROUP)]
-            some = factors[pl.ds(group * GROUP, GROUP), lines_of(half)]
+            some = factors[pl.ds(group * GROUP, GROUP), chosen]
             weighted = dot_nn(some.reshape(GROUP * depth, wide), amps).astype(BF16)
             for q in range(GROUP):
                 total = total + dot_nt(weighted[q * depth:(q + 1) * depth], block[q])
@@ -261,8 +296,9 @@
 
         return lax.fori_loop(0, aux // GROUP, add, jnp.zeros((depth, wide), F32))
 
-    def cycle(first, half):
-        upper, lower = zeta_rows[0, lines_of(half)], zeta_rows[1, lines_of(half)]
+    def cycle(first, start, depth):
+        chosen = pl.ds(pl.multiple_of(start, share), depth)
+        upper, lower = zeta_rows[0, chosen], zeta_rows[1, chosen]
         return dot_nn(upper, ov_mine[first]) + dot_nn(lower, ov_mine[first])
 
     def gather_zeta():
@@ -309,27 +345,23 @@
         def _():
             parts[integ] = hops[which]
 
-    def hand_over(first, half):
-        for step in range(near):
-            row = half * near + lax.rem(virt + 1 + step, near)
-
-            @pl.when(row != virt)
-            def _(row=row):
-                hop_copy(first, row).start()
-
-            @pl.when(row == virt)
-            def _(row=row):
-                hops[virt * held + first] = terms[first, rows(row)]
-                pass_on(virt * held + first)
-
     def work(first):
-        for turn in range(HALVES):
-            half = lax.rem(my_half + 1 + turn, HALVES)
-            total = ladder(first, half)
+        other = lax.rem(my_half + 1, HALVES) * near
+        chunks = [(other, near)]
+        for step in range(1, near + 1):
+            chunks.append((my_half * near + lax.rem(virt + step, near), 1))
+        for turn, (row, count) in enumerate(chunks):
+            total = ladder(first, row * share, count * share)
             if held == 1 and turn == 0:
                 gather_zeta()
-            terms[first, lines_of(half)] = (total + cycle(first, half)).astype(BF16)
-            hand_over(first, half)
+            total = (total + cycle(first, row * share, count * share)).astype(BF16)
+            if turn < near:
+                terms[first, pl.ds(pl.multiple_of(row * share, share), count * share)] = total
+                for offset in range(count):
+                    hop_copy(first, row + offset).start()
+            else:
+                hops[virt * held + first] = total
+                pass_on(virt * held + first)
 
     if held == 1:
         work(0)
@@ -374,6 +406,7 @@
     @pl.when(home == virt)
     def _():
         for step in range(1, planes):
+            domain_copy(step).wait_send()
             ov_copy(step).wait_send()
 
     for first in range(held):
@@ -403,11 +436,10 @@
     dma = pltpu.SemaphoreType.DMA
     return pl.pallas_call(
         functools.partial(kernel, columns, planes),
-        out_shape=jax.ShapeDtypeStruct(amplitudes.shape, BF16),
+        out_shape=pltpu.VMEM(amplitudes.shape, BF16),
         in_specs=[pl.BlockSpec(memory_space=pltpu.HBM)] * 8,
         out_specs=vmem,
         scratch_shapes=[
-            pltpu.VMEM(amplitudes.shape, BF16),
             pltpu.VMEM((ov_factors.shape[0], wide), BF16),
             smem(occ_energy_i.shape, F32),
             smem(occ_energy_j.shape, F32),
@@ -415,7 +447,7 @@
             smem(vv_mask.shape, jnp.int32),
             smem(pair_domain.shape, jnp.int32),
             pltpu.VMEM((aux, wide, wide), BF16),
-            pltpu.VMEM((share, wide), BF16),
+            pltpu.VMEM((held, 8, wide), F32),
             pltpu.VMEM((held, wide, wide), BF16),
             pltpu.VMEM((held, aux, wide), BF16),
             pltpu.VMEM((columns, aux, wide), F32),
@@ -426,6 +458,8 @@
             dma((8,)),
             dma((planes,)),
             dma((planes,)),
+            dma((planes,)),
+            dma((held,)),
             dma((planes,)),
             dma((held,)),
             dma((columns,)),

time: 25.3 us -> 24.1 us (0.953); the launches traced: 24.8 us -> 23.9 us
  local copies, waits for them, and re-layouts: 1.38 us -> 0.62 us
    unnamed x1, local copies, waits for them, and re-layouts: 1.38 us -> 0.62 us
where the time goes in v4:
time: 24.1 us; the launch traced here: 23.9 us
  Pallas kernels  22 us (91%)
  between operations  1.3 us (5%)
  local copies, waits for them, and re-layouts  0.62 us (3%)
    pallas_call x1, Pallas kernels, body(): pl.pallas_call(functools.partial(kernel, columns, planes), out_shape=pltp...  22 us
    unnamed x1, local copies, waits for them, and re-layouts  0.62 us

profile of v4, /device:TPU:0, one launch (start us, length us, event | category | flops | bytes accessed | tf_op | source)
XLA Modules:
  0.0 23.9 jit_solution(3861453573018417893)
XLA Ops:
  1.3 22.0 %shard_map.82 = bf16[1,1,64,256]{3,2,1,0:T(8,128)(2,1)S(1)} custom-call(bf16[1,1,64,256]{3,2,1,0:T(8,128)(2,1)} %amp_hbm.1, bf16[64,256]{1,0:T(8,128)(2,1)} %bitcast.2, f32[1]{0:T(128)S(6)} %copy.11.occ_i_hbm, f32[1]{0:T(128)S(6)} %copy.12.occ_j_hbm, f32[1,256]{1,0:T(1,128)} %bitcast.3, s32[2,2]{1,0:T(2,128)} %vv_mask_hbm.1, s32[1,1,2]{2,1,0:T(1,128)} %domain_hbm.1, ...), custom_call_target="tpu_custom_call" | custom-call | flops 1073741824 | bytes 2097152 | tf_op jit(solution)/shard_map/pallas_call | solution.py:437
  23.3 0.6 %copy.10 = bf16[1,1,64,256]{3,2,1,0:T(8,128)(2,1)} copy(bf16[1,1,64,256]{3,2,1,0:T(8,128)(2,1)S(1)} %shard_map.82) | data formatting | bytes 65536

commit v5 on v4

--- a/solution.py
+++ b/solution.py
@@ -140,9 +140,9 @@
         to_integ = lax.rem(integ + step, planes)
         return remote(
             ov_ref.at[pl.ds(pl.multiple_of(to_integ * aux, aux), aux)],
-            ov_mine.at[slot],
+            ov_mine.at[integ],
             ov_send.at[step],
-            ov_recv.at[slot],
+            ov_recv.at[integ],
             virt,
             to_integ,
         )
@@ -186,8 +186,10 @@
             )
         for step in range(1, planes):
             domain_copy(step).start()
-            ov_copy(step).start()
-        ov_mine[slot] = ov_ref[pl.ds(pl.multiple_of(integ * aux, aux), aux)]
+
+    for step in range(1, planes):
+        ov_copy(step).start()
+    ov_mine[integ] = ov_ref[pl.ds(pl.multiple_of(integ * aux, aux), aux)]
 
     for load in loads[3:7]:
         load.wait()
@@ -213,13 +215,14 @@
     def _(q):
         factors[q] = factors[q] * grid
 
+    def ov_arrived(which):
+        landed = ov_mine.at[which]
+        remote(landed, landed, ov_send.at[0], ov_recv.at[which], virt, integ).wait_recv()
+
     for first in range(held):
         @pl.when(virt * held + first != integ)
         def _(first=first):
-            ov_in = remote(
-                ov_mine.at[first], ov_mine.at[first], ov_send.at[0], ov_recv.at[first], virt, integ
-            )
-            ov_in.wait_recv()
+            ov_arrived(virt * held + first)
             remote(
                 domains.at[first],
                 domains.at[first],
@@ -263,7 +266,8 @@
     zeta_part = jnp.zeros((aux, wide), F32)
     for first in range(held):
         amps = pairs[first]
-        zeta_part += 2.0 * dot_nt(ov_mine[first], amps) - dot_nn(ov_mine[first], amps)
+        ov_own = ov_mine[virt * held + first]
+        zeta_part += 2.0 * dot_nt(ov_own, amps) - dot_nn(ov_own, amps)
     zetas[virt] = zeta_part
 
     def zeta_copy(step):
@@ -295,11 +299,6 @@
             return total
 
         return lax.fori_loop(0, aux // GROUP, add, jnp.zeros((depth, wide), F32))
-
-    def cycle(first, start, depth):
-        chosen = pl.ds(pl.multiple_of(start, share), depth)
-        upper, lower = zeta_rows[0, chosen], zeta_rows[1, chosen]
-        return dot_nn(upper, ov_mine[first]) + dot_nn(lower, ov_mine[first])
 
     def gather_zeta():
         for step in range(1, columns):
@@ -337,6 +336,10 @@
         )
 
     def pass_on(which):
+        upper, lower = zeta_rows[0, rows(virt)], zeta_rows[1, rows(virt)]
+        cycle = dot_nn(upper, ov_mine[which]) + dot_nn(lower, ov_mine[which])
+        hops[which] = (hops[which].astype(F32) + cycle).astype(BF16)
+
         @pl.when(which != integ)
         def _():
             part_copy(which).start()
@@ -352,22 +355,29 @@
             chunks.append((my_half * near + lax.rem(virt + step, near), 1))
         for turn, (row, count) in enumerate(chunks):
             total = ladder(first, row * share, count * share)
-            if held == 1 and turn == 0:
-                gather_zeta()
-            total = (total + cycle(first, row * share, count * share)).astype(BF16)
+            total = total.astype(BF16)
             if turn < near:
                 terms[first, pl.ds(pl.multiple_of(row * share, share), count * share)] = total
                 for offset in range(count):
                     hop_copy(first, row + offset).start()
             else:
                 hops[virt * held + first] = total
-                pass_on(virt * held + first)
 
     if held == 1:
         work(0)
     else:
-        gather_zeta()
         pl.loop(0, held)(work)
+
+    gather_zeta()
+    for first in range(held):
+        for away in range(1, columns):
+            which = lax.rem(virt + away, columns) * held + first
+
+            @pl.when(which != integ)
+            def _(which=which):
+                ov_arrived(which)
+
+        pass_on(virt * held + first)
 
     for turn in range(HALVES):
         half = lax.rem(my_half + 1 + turn, HALVES)
@@ -407,7 +417,9 @@
     def _():
         for step in range(1, planes):
             domain_copy(step).wait_send()
-            ov_copy(step).wait_send()
+
+    for step in range(1, planes):
+        ov_copy(step).wait_send()
 
     for first in range(held):
         for step in range(1, columns):
@@ -449,7 +461,7 @@
             pltpu.VMEM((aux, wide, wide), BF16),
             pltpu.VMEM((held, 8, wide), F32),
             pltpu.VMEM((held, wide, wide), BF16),
-            pltpu.VMEM((held, aux, wide), BF16),
+            pltpu.VMEM((planes, aux, wide), BF16),
             pltpu.VMEM((columns, aux, wide), F32),
             pltpu.VMEM((2, wide, aux), BF16),
             pltpu.VMEM((held, wide, wide), BF16),
@@ -459,7 +471,7 @@
             dma((planes,)),
             dma((planes,)),
             dma((planes,)),
-            dma((held,)),
+            dma((planes,)),
             dma((planes,)),
             dma((held,)),
             dma((columns,)),

time: 24.1 us -> 22.3 us (0.925)
  Pallas kernels: 22 us -> 20.3 us
    pallas_call x1, Pallas kernels: 22 us -> 20.3 us  [body(): pl.pallas_call(functools.partial(kernel, columns, planes), out_shape=pltp...]
where the time goes in v5:
time: 22.3 us; the launch traced here: 22.2 us
  Pallas kernels  20.3 us (91%)
  between operations  1.3 us (6%)
  local copies, waits for them, and re-layouts  0.62 us (3%)
    pallas_call x1, Pallas kernels, body(): pl.pallas_call(functools.partial(kernel, columns, planes), out_shape=pltp...  20.3 us
    unnamed x1, local copies, waits for them, and re-layouts  0.62 us

profile of v5, /device:TPU:0, one launch (start us, length us, event | category | flops | bytes accessed | tf_op | source)
XLA Modules:
  0.0 22.2 jit_solution(14349037564861852763)
XLA Ops:
  1.3 20.3 %shard_map.82 = bf16[1,1,64,256]{3,2,1,0:T(8,128)(2,1)S(1)} custom-call(bf16[1,1,64,256]{3,2,1,0:T(8,128)(2,1)} %amp_hbm.1, bf16[64,256]{1,0:T(8,128)(2,1)} %bitcast.2, f32[1]{0:T(128)S(6)} %copy.11.occ_i_hbm, f32[1]{0:T(128)S(6)} %copy.12.occ_j_hbm, f32[1,256]{1,0:T(1,128)} %bitcast.3, s32[2,2]{1,0:T(2,128)} %vv_mask_hbm.1, s32[1,1,2]{2,1,0:T(1,128)} %domain_hbm.1, ...), custom_call_target="tpu_custom_call" | custom-call | flops 1073741824 | bytes 2097152 | tf_op jit(solution)/shard_map/pallas_call | solution.py:449
  21.6 0.6 %copy.10 = bf16[1,1,64,256]{3,2,1,0:T(8,128)(2,1)} copy(bf16[1,1,64,256]{3,2,1,0:T(8,128)(2,1)S(1)} %shard_map.82) | data formatting | bytes 65536

commit v6 on v5

--- a/solution.py
+++ b/solution.py
@@ -49,6 +49,7 @@
     vv_mask_ref,
     domain_ref,
     factors,
+    turned,
     domains,
     pairs,
     ov_mine,
@@ -213,7 +214,9 @@
 
     @pl.loop(0, aux)
     def _(q):
-        factors[q] = factors[q] * grid
+        kept = factors[q] * grid
+        factors[q] = kept
+        turned[q] = kept.T
 
     def ov_arrived(which):
         landed = ov_mine.at[which]
@@ -291,11 +294,11 @@
         chosen = pl.ds(pl.multiple_of(start, share), depth)
 
         def add(group, total):
-            block = factors[pl.ds(group * GROUP, GROUP)]
+            block = turned[pl.ds(group * GROUP, GROUP)]
             some = factors[pl.ds(group * GROUP, GROUP), chosen]
             weighted = dot_nn(some.reshape(GROUP * depth, wide), amps).astype(BF16)
             for q in range(GROUP):
-                total = total + dot_nt(weighted[q * depth:(q + 1) * depth], block[q])
+                total = total + dot_nn(weighted[q * depth:(q + 1) * depth], block[q])
             return total
 
         return lax.fori_loop(0, aux // GROUP, add, jnp.zeros((depth, wide), F32))
@@ -459,6 +462,7 @@
             smem(vv_mask.shape, jnp.int32),
             smem(pair_domain.shape, jnp.int32),
             pltpu.VMEM((aux, wide, wide), BF16),
+            pltpu.VMEM((aux, wide, wide), BF16),
             pltpu.VMEM((held, 8, wide), F32),
             pltpu.VMEM((held, wide, wide), BF16),
             pltpu.VMEM((planes, aux, wide), BF16),

time: 22.3 us -> 21.8 us (0.978)
  Pallas kernels: 20.3 us -> 19.7 us
    pallas_call x1, Pallas kernels: 20.3 us -> 19.7 us  [body(): pl.pallas_call(functools.partial(kernel, columns, planes), out_shape=pltp...]
where the time goes in v6:
time: 21.8 us; the launch traced here: 21.6 us
  Pallas kernels  19.7 us (90%)
  between operations  1.3 us (6%)
  local copies, waits for them, and re-layouts  0.62 us (3%)
    pallas_call x1, Pallas kernels, body(): pl.pallas_call(functools.partial(kernel, columns, planes), out_shape=pltp...  19.7 us
    unnamed x1, local copies, waits for them, and re-layouts  0.62 us

profile of v6, /device:TPU:0, one launch (start us, length us, event | category | flops | bytes accessed | tf_op | source)
XLA Modules:
  0.0 21.6 jit_solution(13612584817386257863)
XLA Ops:
  1.3 19.7 %shard_map.82 = bf16[1,1,64,256]{3,2,1,0:T(8,128)(2,1)S(1)} custom-call(bf16[1,1,64,256]{3,2,1,0:T(8,128)(2,1)} %amp_hbm.1, bf16[64,256]{1,0:T(8,128)(2,1)} %bitcast.2, f32[1]{0:T(128)S(6)} %copy.11.occ_i_hbm, f32[1]{0:T(128)S(6)} %copy.12.occ_j_hbm, f32[1,256]{1,0:T(1,128)} %bitcast.3, s32[2,2]{1,0:T(2,128)} %vv_mask_hbm.1, s32[1,1,2]{2,1,0:T(1,128)} %domain_hbm.1, ...), custom_call_target="tpu_custom_call" | custom-call | flops 1073741824 | bytes 2097152 | tf_op jit(solution)/shard_map/pallas_call | solution.py:452
  21.0 0.6 %copy.10 = bf16[1,1,64,256]{3,2,1,0:T(8,128)(2,1)} copy(bf16[1,1,64,256]{3,2,1,0:T(8,128)(2,1)S(1)} %shard_map.82) | data formatting | bytes 65536

commit v7 on v6

--- a/solution.py
+++ b/solution.py
@@ -110,12 +110,6 @@
             )
         )
     ]
-    for load in loads[1:]:
-        load.start()
-
-    @pl.when(home == virt)
-    def _():
-        loads[0].start()
 
     barrier = pltpu.get_barrier_semaphore()
 
@@ -134,6 +128,13 @@
             for step in range(1, columns):
                 greet(lax.rem(virt + step, columns), virt * held + first)
 
+    for load in loads[1:]:
+        load.start()
+
+    @pl.when(home == virt)
+    def _():
+        loads[0].start()
+
     away = jnp.where(home != virt, planes - 1, 0)
     pl.semaphore_wait(barrier, planes + columns - 2 + away)
 
@@ -187,9 +188,8 @@
             )
         for step in range(1, planes):
             domain_copy(step).start()
-
-    for step in range(1, planes):
-        ov_copy(step).start()
+            ov_copy(step).start()
+
     ov_mine[integ] = ov_ref[pl.ds(pl.multiple_of(integ * aux, aux), aux)]
 
     for load in loads[3:7]:
@@ -251,6 +251,11 @@
     @pl.when(home == virt)
     def _():
         loads[0].wait()
+
+    @pl.when(home != virt)
+    def _():
+        for step in range(1, planes):
+            ov_copy(step).start()
 
     for first in range(held):
         for upper in range(tiles):

time: 21.8 us -> 21.7 us (level)
  no operation moved by 1% of the time
where the time goes in v7:
time: 21.7 us; the launch traced here: 21.5 us
  Pallas kernels  19.6 us (90%)
  between operations  1.3 us (6%)
  local copies, waits for them, and re-layouts  0.62 us (3%)
    pallas_call x1, Pallas kernels, body(): pl.pallas_call(functools.partial(kernel, columns, planes), out_shape=pltp...  19.6 us
    unnamed x1, local copies, waits for them, and re-layouts  0.62 us

profile of v7, /device:TPU:0, one launch (start us, length us, event | category | flops | bytes accessed | tf_op | source)
XLA Modules:
  0.0 21.5 jit_solution(742179896924411694)
XLA Ops:
  1.3 19.6 %shard_map.82 = bf16[1,1,64,256]{3,2,1,0:T(8,128)(2,1)S(1)} custom-call(bf16[1,1,64,256]{3,2,1,0:T(8,128)(2,1)} %amp_hbm.1, bf16[64,256]{1,0:T(8,128)(2,1)} %bitcast.2, f32[1]{0:T(128)S(6)} %copy.11.occ_i_hbm, f32[1]{0:T(128)S(6)} %copy.12.occ_j_hbm, f32[1,256]{1,0:T(1,128)} %bitcast.3, s32[2,2]{1,0:T(2,128)} %vv_mask_hbm.1, s32[1,1,2]{2,1,0:T(1,128)} %domain_hbm.1, ...), custom_call_target="tpu_custom_call" | custom-call | flops 1073741824 | bytes 2097152 | tf_op jit(solution)/shard_map/pallas_call | solution.py:457
  20.9 0.6 %copy.10 = bf16[1,1,64,256]{3,2,1,0:T(8,128)(2,1)} copy(bf16[1,1,64,256]{3,2,1,0:T(8,128)(2,1)S(1)} %shard_map.82) | data formatting | bytes 65536

commit v8 on v7

--- a/solution.py
+++ b/solution.py
@@ -8,7 +8,7 @@
 from jax.sharding import PartitionSpec as P
 
 TILE_SIZE = 128
-GROUP = 8
+GROUP = 16
 HALVES = 2
 MESH = pl.DeviceIdType.MESH
 F32 = jnp.float32

time: 21.7 us -> 21.5 us (level)
  no operation moved by 1% of the time
where the time goes in v8:
time: 21.5 us; the launch traced here: 21.4 us
  Pallas kernels  19.4 us (90%)
  between operations  1.3 us (6%)
  local copies, waits for them, and re-layouts  0.62 us (3%)
    pallas_call x1, Pallas kernels, body(): pl.pallas_call(functools.partial(kernel, columns, planes), out_shape=pltp...  19.4 us
    unnamed x1, local copies, waits for them, and re-layouts  0.62 us

profile of v8, /device:TPU:0, one launch (start us, length us, event | category | flops | bytes accessed | tf_op | source)
XLA Modules:
  0.0 21.4 jit_solution(8922021609366432818)
XLA Ops:
  1.3 19.4 %shard_map.82 = bf16[1,1,64,256]{3,2,1,0:T(8,128)(2,1)S(1)} custom-call(bf16[1,1,64,256]{3,2,1,0:T(8,128)(2,1)} %amp_hbm.1, bf16[64,256]{1,0:T(8,128)(2,1)} %bitcast.2, f32[1]{0:T(128)S(6)} %copy.11.occ_i_hbm, f32[1]{0:T(128)S(6)} %copy.12.occ_j_hbm, f32[1,256]{1,0:T(1,128)} %bitcast.3, s32[2,2]{1,0:T(2,128)} %vv_mask_hbm.1, s32[1,1,2]{2,1,0:T(1,128)} %domain_hbm.1, ...), custom_call_target="tpu_custom_call" | custom-call | flops 1073741824 | bytes 2097152 | tf_op jit(solution)/shard_map/pallas_call | solution.py:457
  20.7 0.6 %copy.10 = bf16[1,1,64,256]{3,2,1,0:T(8,128)(2,1)} copy(bf16[1,1,64,256]{3,2,1,0:T(8,128)(2,1)S(1)} %shard_map.82) | data formatting | bytes 65536

commit v9 on v8

--- a/solution.py
+++ b/solution.py
@@ -358,13 +358,13 @@
 
     def work(first):
         other = lax.rem(my_half + 1, HALVES) * near
-        chunks = [(other, near)]
+        chunks = [(other + offset, 1) for offset in range(near)]
         for step in range(1, near + 1):
             chunks.append((my_half * near + lax.rem(virt + step, near), 1))
         for turn, (row, count) in enumerate(chunks):
             total = ladder(first, row * share, count * share)
             total = total.astype(BF16)
-            if turn < near:
+            if turn < len(chunks) - 1:
                 terms[first, pl.ds(pl.multiple_of(row * share, share), count * share)] = total
                 for offset in range(count):
                     hop_copy(first, row + offset).start()

time: 21.5 us -> 22.2 us (1.033)
  Pallas kernels: 19.4 us -> 20.1 us
    pallas_call x1, Pallas kernels: 19.4 us -> 20.1 us  [body(): pl.pallas_call(functools.partial(kernel, columns, planes), out_shape=pltp...]
where the time goes in v9:
time: 22.2 us; the launch traced here: 22 us
  Pallas kernels  20.1 us (91%)
  between operations  1.3 us (6%)
  local copies, waits for them, and re-layouts  0.62 us (3%)
    pallas_call x1, Pallas kernels, body(): pl.pallas_call(functools.partial(kernel, columns, planes), out_shape=pltp...  20.1 us
    unnamed x1, local copies, waits for them, and re-layouts  0.62 us

profile of v9, /device:TPU:0, one launch (start us, length us, event | category | flops | bytes accessed | tf_op | source)
XLA Modules:
  0.0 22.0 jit_solution(6517605074806864574)
XLA Ops:
  1.3 20.1 %shard_map.82 = bf16[1,1,64,256]{3,2,1,0:T(8,128)(2,1)S(1)} custom-call(bf16[1,1,64,256]{3,2,1,0:T(8,128)(2,1)} %amp_hbm.1, bf16[64,256]{1,0:T(8,128)(2,1)} %bitcast.2, f32[1]{0:T(128)S(6)} %copy.11.occ_i_hbm, f32[1]{0:T(128)S(6)} %copy.12.occ_j_hbm, f32[1,256]{1,0:T(1,128)} %bitcast.3, s32[2,2]{1,0:T(2,128)} %vv_mask_hbm.1, s32[1,1,2]{2,1,0:T(1,128)} %domain_hbm.1, ...), custom_call_target="tpu_custom_call" | custom-call | flops 1073741824 | bytes 2097152 | tf_op jit(solution)/shard_map/pallas_call | solution.py:457
  21.4 0.6 %copy.10 = bf16[1,1,64,256]{3,2,1,0:T(8,128)(2,1)} copy(bf16[1,1,64,256]{3,2,1,0:T(8,128)(2,1)S(1)} %shard_map.82) | data formatting | bytes 65536
